TPU v7x, 512 devices: a whole 4x8x8 slice. The times are simulated.
512 devices in a mesh: dp: 16 (over y, core), seq: 32 (over x, z).
Axes of the slice: x: 4, y: 8, z: 8, core: 2. Of those that a mesh axis runs over, the one named last changes fastest.
Arguments:
- frame_in: bfloat16 [16, 4608, 1024], P('dp', 'seq'), may hold values from -120 to 120
- token_ids: int32 [16, 32, 60], P('dp', 'seq'), may hold values from 0 to 3327
- durations: int32 [16, 32, 60], P('dp', 'seq'), may hold values from 1 to 4, 144 in all within a row
- valid_len: int32 [16], P('dp'), may hold values from 1152 to 4608, as said below
- t_bin: int32 [16], P('dp'), may hold values from 0 to 63
- token_table: bfloat16 [3328, 512], P('seq'), may hold values from -6 to 6
- enc_weight: bfloat16 [512, 1024], replicated, may hold values from -0.25 to 0.25
- mod_table: float32 [64, 2048], replicated, may hold values from -1.2 to 2.5
- w_query: bfloat16 [1024, 512], P('seq'), may hold values from -0.1875 to 0.1875
- w_key: bfloat16 [1024, 512], P('seq'), may hold values from -0.1875 to 0.1875
- w_value: bfloat16 [1024, 512], P('seq'), may hold values from -0.1875 to 0.1875
- attn_grad: bfloat16 [16, 4608, 512], P('dp', 'seq'), may hold values from -6 to 6
Outputs:
- attn_out: bfloat16 [16, 4608, 512], P('dp', 'seq')
- frame_grad: bfloat16 [16, 4608, 1024], P('dp', 'seq')
- query_weight_grad: float32 [1024, 512], P('seq')
- key_weight_grad: float32 [1024, 512], P('seq')
- value_weight_grad: float32 [1024, 512], P('seq')
Inputs may be any that keep to these rules, and one draw needn't show every extreme that they name: In every slab the 60 durations sum to 144, so each token's frames lie in its own slab; some token lasts 4 frames. `valid_len`: some recording is valid over all 4608 frames.
All inputs are finite; a program needn't handle non-finite values.
Results may differ from a plain program's by a relative error of at most 0.017.
The roundings to bfloat16 on the way count: a program that leaves them out, or rounds other values in their place, can miss the bound.
Values may be sent and summed in bfloat16 or wider, within the bound.
A program may use at most 64 MiB of HBM per device.

v0:
```python
import math
import jax
import jax.numpy as jnp
from jax import lax
from jax.sharding import PartitionSpec as P

D = 1024
HEADS = 8
HD = 64
BLK = 48
QW = 512


def extended_2(cells, sides, width):
    for axis, dim in sides:
        count = lax.axis_size(axis)
        ends = count - 1
        head = lax.slice_in_dim(cells, 0, width, axis=dim)
        tail = lax.slice_in_dim(cells, cells.shape[dim] - width, cells.shape[dim], axis=dim)
        cells = jnp.concatenate(
            [
                lax.ppermute(tail, axis, [(i, (i + 1) % count) for i in range(ends)]),
                cells,
                lax.ppermute(head, axis, [((i + 1) % count, i) for i in range(ends)]),
            ],
            axis=dim,
        )
    return cells


def shifted(block, axis, distance):
    devices = range(lax.axis_size(axis))
    route = [(i - distance, i) for i in devices if i - distance in devices]
    return lax.ppermute(block, axis, route)


def attend_window(
    q_blocks, key_ext, value_ext, grad_out, query_pos, key_pos, valid_end, frames_total
):
    n_blocks = q_blocks.shape[0]
    block_len = q_blocks.shape[1]
    key_win = jnp.concatenate([key_ext[offset : offset + n_blocks] for offset in range(4)], axis=1)
    value_win = jnp.concatenate(
        [value_ext[offset : offset + n_blocks] for offset in range(4)], axis=1
    )
    key_here = key_pos[:, None, :]
    allowed = (
        (key_here >= 0)
        & (key_here < frames_total)
        & ((key_here < valid_end) | (query_pos[:, :, None] >= valid_end))
    )
    row_mask = allowed[:, None]
    inv_scale = 1.0 / math.sqrt(q_blocks.shape[-1])
    scores = (
        jnp.einsum("bqhd,bkhd->bhqk", q_blocks, key_win, preferred_element_type=jnp.float32)
        * inv_scale
    )
    scores = jnp.where(row_mask, scores, -1e30)
    row_top = jnp.max(scores, axis=-1, keepdims=True)
    shifted_exp = jnp.where(row_mask, jnp.exp(scores - row_top), 0.0)
    attn_prob = shifted_exp / jnp.sum(shifted_exp, axis=-1, keepdims=True)
    probs_low = attn_prob.astype(jnp.bfloat16)
    mixed_out = jnp.einsum(
        "bhqk,bkhd->bqhd", probs_low, value_win, preferred_element_type=jnp.float32
    ).astype(jnp.bfloat16)
    grad_probs = jnp.einsum(
        "bqhd,bkhd->bhqk", grad_out, value_win, preferred_element_type=jnp.float32
    )
    centre = jnp.sum(attn_prob * grad_probs, axis=-1, keepdims=True)
    grad_scores = (attn_prob * (grad_probs - centre) * inv_scale).astype(jnp.bfloat16)
    grad_query = jnp.einsum(
        "bhqk,bkhd->bqhd", grad_scores, key_win, preferred_element_type=jnp.float32
    ).astype(jnp.bfloat16)
    key_terms = jnp.einsum(
        "bhqk,bqhd->bkhd", grad_scores, q_blocks, preferred_element_type=jnp.float32
    )
    value_terms = jnp.einsum(
        "bhqk,bqhd->bkhd", probs_low, grad_out, preferred_element_type=jnp.float32
    )
    win_terms = jnp.concatenate([key_terms, value_terms], axis=2)
    pieces = win_terms.reshape(n_blocks, 4, block_len, win_terms.shape[2], win_terms.shape[3])
    folded = jnp.zeros((n_blocks + 3,) + pieces.shape[2:], jnp.float32)
    for offset in range(4):
        folded = folded + jnp.pad(pieces[:, offset], ((offset, 3 - offset), (0, 0), (0, 0), (0, 0)))
    return (mixed_out, grad_query, folded)


def pick_rows(wanted, table_piece):
    inside = (wanted >= 0) & (wanted < table_piece.shape[0])
    picked = jnp.take(table_piece, jnp.clip(wanted, 0, table_piece.shape[0] - 1), axis=0)
    return jnp.where(inside[:, None], picked, jnp.zeros_like(picked))


def shards(
    frame_in,
    token_ids,
    durations,
    valid_len,
    t_bin,
    token_table,
    enc_weight,
    mod_table,
    w_query,
    w_key,
    w_value,
    attn_grad,
):
    frames = frame_in[0]
    n_frames = frames.shape[0]
    seq_count = lax.axis_size("seq")
    seq_index = lax.axis_index("seq")
    dp_count = lax.axis_size("dp")
    frames_total = n_frames * seq_count
    valid_end = valid_len[0]
    wanted = token_ids[0, 0]
    token_emb = pick_rows(wanted, lax.all_gather(token_table, "seq", axis=0, tiled=True))
    token_ends = jnp.cumsum(durations[0, 0])
    local_pos = jnp.arange(n_frames, dtype=jnp.int32)
    owner_tok = jnp.sum((token_ends[None, :] <= local_pos[:, None]).astype(jnp.int32), axis=1)
    frame_emb = jnp.take(token_emb, owner_tok, axis=0)
    hidden_in = frames.astype(jnp.float32) + jnp.dot(
        frame_emb, enc_weight, preferred_element_type=jnp.float32
    )
    root_ms = jnp.sqrt(jnp.mean(hidden_in * hidden_in, axis=1, keepdims=True) + 1e-06)
    normed = hidden_in / root_ms
    modulation = lax.dynamic_index_in_dim(mod_table, t_bin[0], 0, keepdims=False)
    gain_part = 1.0 + modulation[:D]
    shift_part = modulation[D:]
    modulated = (normed * gain_part + shift_part).astype(jnp.bfloat16)
    shard_cat = jnp.concatenate([w_query, w_key, w_value], axis=1)
    weights_all = lax.all_gather(shard_cat, "seq", axis=0, tiled=True)
    projected = jnp.dot(modulated, weights_all, preferred_element_type=jnp.float32).astype(
        jnp.bfloat16
    )
    queries = projected[:, :QW]
    keys_values = projected[:, QW:]
    padded = extended_2(keys_values, (("seq", 0),), 2 * BLK)
    extended = padded[: n_frames + 3 * BLK]
    n_blocks = n_frames // BLK
    ext_blocks = extended.reshape(n_blocks + 3, BLK, 2, HEADS, HD)
    global_pos = seq_index * n_frames + local_pos
    query_pos = global_pos.reshape(n_blocks, BLK)
    key_pos = (
        seq_index * n_frames
        + (jnp.arange(n_blocks, dtype=jnp.int32)[:, None] - 2) * BLK
        + jnp.arange(4 * BLK, dtype=jnp.int32)[None, :]
    )
    live_rows = global_pos < valid_end
    grad_live = jnp.where(live_rows[:, None], attn_grad[0], jnp.zeros_like(attn_grad[0]))
    attn_blocks, query_grad, ext_grad = attend_window(
        queries.reshape(n_blocks, BLK, HEADS, HD),
        ext_blocks[:, :, 0],
        ext_blocks[:, :, 1],
        grad_live.reshape(n_blocks, BLK, HEADS, HD),
        query_pos,
        key_pos,
        valid_end,
        frames_total,
    )
    ext_rows = ext_grad.reshape(n_frames + 3 * BLK, 2 * QW)
    from_next = shifted(ext_rows[: 2 * BLK], "seq", -1)
    from_prev = shifted(ext_rows[n_frames + 2 * BLK :], "seq", 1)
    own_rows = ext_rows[2 * BLK : 2 * BLK + n_frames]
    own_rows = (
        own_rows
        + jnp.pad(from_next, ((n_frames - 2 * BLK, 0), (0, 0)))
        + jnp.pad(from_prev, ((0, n_frames - BLK), (0, 0)))
    )
    grad_cat = jnp.concatenate(
        [query_grad.reshape(n_frames, QW), own_rows.astype(jnp.bfloat16)], axis=1
    )
    grad_scale = 1.0 / math.sqrt(dp_count * frames_total)
    per_seq = lax.psum_scatter(
        (
            lax.dot_general(
                modulated, grad_cat, (((0,), (0,)), ((), ())), preferred_element_type=jnp.float32
            )
            * grad_scale
        ).astype(jnp.bfloat16),
        "seq",
        scatter_dimension=0,
        tiled=True,
    ).astype(jnp.float32)
    weight_grad = lax.psum(per_seq, "dp")
    hidden_grad = lax.dot_general(
        grad_cat, weights_all, (((1,), (1,)), ((), ())), preferred_element_type=jnp.float32
    )
    scaled_grad = hidden_grad * gain_part
    frame_grad = (
        scaled_grad - normed * jnp.mean(scaled_grad * normed, axis=1, keepdims=True)
    ) / root_ms
    return (
        attn_blocks.reshape(n_frames, QW)[None],
        frame_grad.astype(jnp.bfloat16)[None],
        weight_grad[:, :QW],
        weight_grad[:, QW : 2 * QW],
        weight_grad[:, 2 * QW :],
    )


def solution(mesh):
    placed = (
        P("dp", "seq", None),
        P("dp", "seq", None),
        P("dp", "seq", None),
        P("dp"),
        P("dp"),
        P("seq", None),
        P(),
        P(),
        P("seq", None),
        P("seq", None),
        P("seq", None),
        P("dp", "seq", None),
    )
    return jax.shard_map(
        shards,
        mesh=mesh,
        in_specs=placed,
        out_specs=(
            P("dp", "seq", None),
            P("dp", "seq", None),
            P("seq", None),
            P("seq", None),
            P("seq", None),
        ),
        check_vma=False,
    )
```

profile of v0, /device:TPU:25, one launch (start us, length us, event | category | flops | bytes accessed | tf_op | source)
XLA Modules:
  0.0 553.6 jit_solution(4595249403937196069)
XLA Ops:
  11.8 1.9 squeeze.30
  16.7 81.7 %all-gather.3.cloned.1.call-done = bf16[3328,512]{1,0:T(8,128)(2,1)} async-done(((bf16[104,512]{1,0:T(8,128)(2,1)}), bf16[3328,512]{1,0:T(8,128)(2,1)}) %all-gather.3.cloned.1.call-update) | async-done | bytes 3407888 | tf_op jit(solution)/shard_map/all_gather | solution.py:116
  98.5 3.1 gather_fusion
  103.1 81.1 %all-gather.5.cloned.1.call-done = bf16[1024,1536]{1,0:T(8,128)(2,1)} async-done(((bf16[32,1536]{1,0:T(8,128)(2,1)}), bf16[1024,1536]{1,0:T(8,128)(2,1)}) %all-gather.5.cloned.1.call-update) | async-done | bytes 3145744 | tf_op jit(solution)/shard_map/all_gather | solution.py:131
  184.2 2.6 convolution_convert_fusion
  186.8 2.8 collective-permute-start
  192.3 3.8 collective-permute-done.1
  199.6 2.1 copy.74
  206.2 3.3 fusion.56
  209.5 2.1 convolution_bitcast_fusion
  211.6 2.0 fusion.24
  213.6 10.4 %convolution_bitcast_fusion.1 = f32[3,192,8,64]{1,3,2,0:T(8,128)} fusion(f32[3,8,48,192]{3,2,1,0:T(8,128)} %fusion.24, bf16[3,48,8,64]{3,2,1,0:T(8,128)(2,1)} %reshape.221, f32[3,8,48,192]{3,2,1,0:T(8,128)} %get-tuple-element.29, f32[3,8,48]{2,1,0:T(8,128)S(1)} %get-tuple-element.28), kind=kOutput, calls=%fused_computation.10 | convolution fusion | flops 29861184 | bytes 3101184 | tf_op jit(solution)/shard_map/bhqk,bqhd->bkhd/dot_general | solution.py:74
  224.0 3.5 pad_maximum_fusion
  227.5 5.9 %copy.64 = f32[3,192,16,64]{3,2,1,0:T(8,128)} copy(f32[3,192,16,64]{1,3,2,0:T(8,128)} %pad_maximum_fusion) | data formatting | bytes 4718592 | tf_op jit(solution)/shard_map/concatenate | solution.py:80
  233.4 2.7 slice_bitcast_fusion.3
  240.0 2.2 slice.152
  244.6 1.8 slice.154
  246.4 4.5 collective-permute-start.3
  250.9 10.3 %fusion.11 = bf16[3,48,8,64]{3,1,2,0:T(8,128)(2,1)S(1)} fusion(f32[3,8,48,192]{3,2,1,0:T(8,128)} %fusion.24, bf16[3,48,8,64]{1,3,2,0:T(8,128)(2,1)} %bitcast.85, bf16[3,48,8,64]{1,3,2,0:T(8,128)(2,1)} %bitcast.80, bf16[3,48,8,64]{1,3,2,0:T(8,128)(2,1)} %bitcast.83, bf16[3,48,8,64]{1,3,2,0:T(8,128)(2,1)} %bitcast.79, ...), kind=kOutput, calls=%fused_computation.28 | convolution fusion | flops 32294208 | bytes 2511360 | tf_op jit(solution)/shard_map/bhqk,bkhd->bqhd/dot_general | solution.py:71
  263.8 2.7 multiply_convert_fusion
  267.9 2.2 fusion.10
  271.0 3.3 multiply_reduce_fusion.1
  275.2 218.2 %reduce-scatter.2.cloned.1.call-done = bf16[32,1536]{1,0:T(8,128)(2,1)} async-done(((bf16[1024,1536]{1,0:T(8,128)(2,1)}), bf16[32,1536]{1,0:T(8,128)(2,1)}) %reduce-scatter.2.cloned.1.call-update) | async-done | bytes 98320 | tf_op jit(solution)/shard_map/reduce_scatter | solution.py:173
  493.4 53.0 %all-reduce.7 = f32[32,1536]{1,0:T(8,128)S(1)} all-reduce(bf16[32,1536]{1,0:T(8,128)(2,1)} %reduce-scatter.2.cloned.1.call-done), channel_id=1, replica_groups=mesh['dp'=16,'seq'=32] {'dp'}, use_global_device_ids=true, to_apply=%region_8.9 | all-reduce | flops 49152 | bytes 294912 | tf_op jit(solution)/shard_map/psum | solution.py:184
  (130 shorter events, 31.1 us)
Async XLA Ops:
  7.2 95.4 %copy-start = (bf16[512,1024]{1,0:T(8,128)(2,1)S(1)}, bf16[512,1024]{1,0:T(8,128)(2,1)}, u32[]{:S(2)}) copy-start(bf16[512,1024]{1,0:T(8,128)(2,1)} %param.18) | copy-start | bytes 3145732
  7.2 91.3 %all-gather.3.cloned.1.call-start = ((), (), s32[]{:S(2)}) async-start(), calls=%async_computation.1 | async-start | bytes 3514368 | tf_op jit(solution)/shard_map/all_gather | solution.py:116
  7.9 176.3 %all-gather.5.cloned.1.call-start = ((), (), s32[]{:S(2)}) async-start(), calls=%async_computation.2 | async-start | bytes 3244032 | tf_op jit(solution)/shard_map/all_gather | solution.py:131
  9.4 484.0 %reduce-scatter.2.cloned.1.call-start = ((), (), s32[]{:S(2)}) async-start(), calls=%async_computation.3 | async-start | bytes 3244032 | tf_op jit(solution)/shard_map/reduce_scatter | solution.py:173
  11.7 90.8 %copy-start.22 = (bf16[1,144,1024]{2,1,0:T(8,128)(2,1)S(1)}, bf16[1,144,1024]{2,1,0:T(8,128)(2,1)}, u32[]{:S(2)}) copy-start(bf16[1,144,1024]{2,1,0:T(8,128)(2,1)} %param.12) | copy-start | bytes 884740
  15.3 168.9 %copy-start.24 = (f32[1,1024]{1,0:T(1,128)}, f32[1,1024]{1,0:T(1,128)S(1)}, u32[]{:S(2)}) copy-start(f32[1,1024]{1,0:T(1,128)S(1)} %get-tuple-element.17) | copy-start | bytes 12292
  15.3 168.9 %copy-start.27 = (f32[1,1024]{1,0:T(1,128)}, f32[1,1024]{1,0:T(1,128)S(1)}, u32[]{:S(2)}) copy-start(f32[1,1024]{1,0:T(1,128)S(1)} %get-tuple-element.18) | copy-start | bytes 12292
  103.1 83.7 %copy-start.6 = (f32[144,1024]{1,0:T(8,128)}, f32[144,1024]{1,0:T(8,128)S(1)}, u32[]{:S(2)}) copy-start(f32[144,1024]{1,0:T(8,128)S(1)} %get-tuple-element.27) | copy-start | bytes 1769476
  103.1 81.1 %copy-start.29 = (f32[144]{0:T(256)}, f32[144]{0:T(256)S(1)}, u32[]{:S(2)}) copy-start(f32[144]{0:T(256)S(1)} %add_sqrt_fusion) | copy-start | bytes 1732
  186.8 5.4 collective-permute-start
  189.7 6.4 %collective-permute-start.1 = (bf16[96,1024]{1,0:T(8,128)(2,1)S(1)}, bf16[96,1024]{1,0:T(8,128)(2,1)S(1)}, u32[]{:S(2)}, u32[]{:S(2)}) collective-permute-start(bf16[96,1024]{1,0:T(8,128)(2,1)S(1)} %get-tuple-element.20), channel_id=1, source_target_pairs={{1,0},{2,1},{3,2},{4,3},{5,4},{6,5},{7,6},{8,7},{9,8},{10,9},{11,1... | collective-permute-start | bytes 589832 | tf_op jit(solution)/shard_map/ppermute | solution.py:24
  198.3 3.3 copy-start.9
  198.3 4.3 copy-start.8
  199.6 6.6 %copy-start.18 = (bf16[3,48,1,8,64]{1,4,3,0,2:T(8,128)(2,1)}, bf16[3,48,1,8,64]{1,4,3,0,2:T(8,128)(2,1)S(1)}, u32[]{:S(2)}) copy-start(bf16[3,48,1,8,64]{1,4,3,0,2:T(8,128)(2,1)S(1)} %copy.72) | copy-start | bytes 442372
  204.9 6.7 %copy-start.14 = (bf16[3,48,1,8,64]{1,4,3,0,2:T(8,128)(2,1)}, bf16[3,48,1,8,64]{1,4,3,0,2:T(8,128)(2,1)S(1)}, u32[]{:S(2)}) copy-start(bf16[3,48,1,8,64]{1,4,3,0,2:T(8,128)(2,1)S(1)} %copy.69) | copy-start | bytes 442372
  206.2 3.3 copy-start.20
  209.5 4.1 copy-start.32
  242.1 19.7 %collective-permute-start.2 = (f32[96,1024]{1,0:T(8,128)}, f32[96,1024]{1,0:T(8,128)}, u32[]{:S(2)}, u32[]{:S(2)}) collective-permute-start(f32[96,1024]{1,0:T(8,128)} %slice.152), channel_id=1, source_target_pairs={{1,0},{2,1},{3,2},{4,3},{5,4},{6,5},{7,6},{8,7},{9,8},{10,9},{11,1... | collective-permute-start | bytes 1179656 | tf_op jit(solution)/shard_map/ppermute | solution.py:34
  243.8 7.1 %copy-start.33 = (f32[3,8,48]{2,1,0:T(8,128)S(1)}, f32[3,8,48]{2,1,0:T(8,128)}, u32[]{:S(2)}) copy-start(f32[3,8,48]{2,1,0:T(8,128)} %copy-done.32) | copy-start | bytes 13828
  246.4 15.5 %collective-permute-start.3 = (f32[48,1024]{1,0:T(8,128)}, f32[48,1024]{1,0:T(8,128)}, u32[]{:S(2)}, u32[]{:S(2)}) collective-permute-start(f32[48,1024]{1,0:T(8,128)} %slice.154), channel_id=1, source_target_pairs={{0,1},{1,2},{2,3},{3,4},{4,5},{5,6},{6,7},{7,8},{8,9},{9,10},{10,1... | collective-permute-start | bytes 589832 | tf_op jit(solution)/shard_map/ppermute | solution.py:34
  250.9 10.6 %slice-start = ((f32[6,48,16,64]{3,2,1,0:T(8,128)}), f32[3,48,16,64]{3,2,1,0:T(8,128)S(1)}, s32[]{:S(2)}) async-start(f32[6,48,16,64]{3,2,1,0:T(8,128)} %copy-done.5), calls=%async_computation.4 | async-start | bytes 2359296 | tf_op jit(solution)/shard_map/slice | solution.py:163
  261.4 2.3 copy-start.7
  267.9 3.2 copy-start.26
  267.9 3.2 copy-start.31
  (19 other events, 29.5 us)
Sparse Core Ops, SparseCore 0:
  11.2 87.2 all-gather.2
  102.2 81.9 all-gather.4
  266.7 226.6 reduce-scatter.1
where the time goes:
time: 555 us; the launch traced here: 554 us
  waiting for transfers between devices  386 us (70%)
  blocking collectives  53 us (10%)
  matrix products  39.3 us (7%)
  local copies, waits for them, and re-layouts  38.3 us (7%)
  between operations  15.5 us (3%)
  other arithmetic  11.6 us (2%)
  starting transfers between devices  10.3 us (2%)
    reduce_scatter x1, waiting for transfers between devices, shards(): lax.psum_scatter((lax.dot_general(modulated, grad_cat, (((0,), (0,)), (()...  218 us
    all_gather x1, waiting for transfers between devices, shards(): lax.all_gather(token_table, 'seq', axis=0, tiled=True)  81.7 us
    all_gather x1, waiting for transfers between devices, shards(): weights_all = lax.all_gather(shard_cat, 'seq', axis=0, tiled=True)  81.1 us
    psum x1, blocking collectives, shards(): weight_grad = lax.psum(per_seq, 'dp')  53 us
    unnamed x78, local copies, waits for them, and re-layouts  12.7 us
  transfers between devices with their start and end apart: 7, of which 4 were waited for; matrix products, arithmetic and copies ran while one was open for 6% of the time, Pallas kernels for 0%

commit v1 on v0

--- a/solution.py
+++ b/solution.py
@@ -128,7 +128,9 @@
     shift_part = modulation[D:]
     modulated = (normed * gain_part + shift_part).astype(jnp.bfloat16)
     shard_cat = jnp.concatenate([w_query, w_key, w_value], axis=1)
-    weights_all = lax.all_gather(shard_cat, "seq", axis=0, tiled=True)
+    weights_all = jnp.concatenate(
+        lax.all_to_all(jnp.stack([shard_cat] * lax.axis_size("seq")), "seq", 0, 0), axis=0
+    )
     projected = jnp.dot(modulated, weights_all, preferred_element_type=jnp.float32).astype(
         jnp.bfloat16
     )

time: 555 us -> 495 us (0.89)
  waiting for transfers between devices: 386 us -> 314 us
  starting transfers between devices: 10.3 us -> 23.1 us
    all_gather x1 -> x0, waiting for transfers between devices: 81.1 us -> none  [shards(): weights_all = lax.all_gather(shard_cat, 'seq', axis=0, tiled=True)]
    all_to_all x0 -> x1, starting transfers between devices: none -> 13.1 us  [shards(): lax.all_to_all(jnp.stack([shard_cat] * lax.axis_size('seq')), 'seq', 0, 0)]
    all_gather x1, waiting for transfers between devices: 81.7 us -> 91.2 us  [shards(): lax.all_gather(token_table, 'seq', axis=0, tiled=True)]
    unnamed x78 -> x84, local copies, waits for them, and re-layouts: 12.7 us -> 13.3 us
  transfers between devices with their start and end apart: 7 -> 7, of which waited for: 4 -> 3; matrix products, arithmetic and copies ran while one was open for 6% -> 6% of each run, Pallas kernels for 0% -> 0%
where the time goes in v1:
time: 495 us; the launch traced here: 494 us
  waiting for transfers between devices  314 us (63%)
  blocking collectives  53.1 us (11%)
  local copies, waits for them, and re-layouts  39.4 us (8%)
  matrix products  39.3 us (8%)
  starting transfers between devices  23.1 us (5%)
  between operations  15.9 us (3%)
  other arithmetic  8.97 us (2%)
    reduce_scatter x1, waiting for transfers between devices, shards(): lax.psum_scatter((lax.dot_general(modulated, grad_cat, (((0,), (0,)), (()...  218 us
    all_gather x1, waiting for transfers between devices, shards(): lax.all_gather(token_table, 'seq', axis=0, tiled=True)  91.2 us
    psum x1, blocking collectives, shards(): weight_grad = lax.psum(per_seq, 'dp')  53.1 us
    unnamed x84, local copies, waits for them, and re-layouts  13.3 us
    all_to_all x1, starting transfers between devices, shards(): lax.all_to_all(jnp.stack([shard_cat] * lax.axis_size('seq')), 'seq', 0, 0)  13.1 us
    dot_general x1, matrix products, attend_window(): jnp.einsum('bhqk,bqhd->bkhd', grad_scores, q_blocks, preferred_element_ty...  10.5 us
    dot_general x1, matrix products, attend_window(): jnp.einsum('bhqk,bkhd->bqhd', grad_scores, key_win, preferred_element_typ...  10.3 us
  transfers between devices with their start and end apart: 7, of which 3 were waited for; matrix products, arithmetic and copies ran while one was open for 6% of the time, Pallas kernels for 0%

profile of v1, /device:TPU:25, one launch (start us, length us, event | category | flops | bytes accessed | tf_op | source)
XLA Modules:
  0.0 493.8 jit_solution(15608763390817869144)
XLA Ops:
  8.7 2.1 stack.2
  10.8 13.1 %all-to-all-start = ((bf16[32,32,1536]{2,1,0:T(8,128)(2,1)}), bf16[32,32,1536]{2,1,0:T(8,128)(2,1)}, u32[]{:S(2)}, u32[]{:S(2)}) async-start(bf16[32,32,1536]{2,1,0:T(8,128)(2,1)} %stack.2), calls=%async_computation | async-start | bytes 6291456 | tf_op jit(solution)/shard_map/all_to_all | solution.py:132
  27.8 91.2 %all-gather.2.cloned.1.call-done = bf16[3328,512]{1,0:T(8,128)(2,1)} async-done(((bf16[104,512]{1,0:T(8,128)(2,1)}), bf16[3328,512]{1,0:T(8,128)(2,1)}) %all-gather.2.cloned.1.call-update) | async-done | bytes 3407888 | tf_op jit(solution)/shard_map/all_gather | solution.py:116
  118.9 3.1 gather_fusion
  124.2 2.6 convolution_convert_fusion
  126.8 2.2 collective-permute-start
  131.6 4.2 collective-permute-done.1
  139.3 2.1 copy.74
  145.9 3.3 fusion.56
  149.2 2.1 convolution_bitcast_fusion
  151.3 2.0 fusion.24
  153.3 10.5 %convolution_bitcast_fusion.1 = f32[3,192,8,64]{1,3,2,0:T(8,128)} fusion(f32[3,8,48,192]{3,2,1,0:T(8,128)} %fusion.24, bf16[3,48,8,64]{3,2,1,0:T(8,128)(2,1)} %reshape.227, f32[3,8,48,192]{3,2,1,0:T(8,128)} %get-tuple-element.29, f32[3,8,48]{2,1,0:T(8,128)S(1)} %get-tuple-element.28), kind=kOutput, calls=%fused_computation.10 | convolution fusion | flops 29861184 | bytes 3101184 | tf_op jit(solution)/shard_map/bhqk,bqhd->bkhd/dot_general | solution.py:74
  163.7 3.5 pad_maximum_fusion
  167.2 5.9 %copy.64 = f32[3,192,16,64]{3,2,1,0:T(8,128)} copy(f32[3,192,16,64]{1,3,2,0:T(8,128)} %pad_maximum_fusion) | data formatting | bytes 4718592 | tf_op jit(solution)/shard_map/concatenate | solution.py:80
  173.1 2.7 slice_bitcast_fusion.3
  179.7 2.1 slice.152
  184.3 1.8 slice.154
  186.1 4.8 collective-permute-start.3
  190.8 10.3 %fusion.11 = bf16[3,48,8,64]{3,1,2,0:T(8,128)(2,1)S(1)} fusion(f32[3,8,48,192]{3,2,1,0:T(8,128)} %fusion.24, bf16[3,48,8,64]{1,3,2,0:T(8,128)(2,1)} %bitcast.86, bf16[3,48,8,64]{1,3,2,0:T(8,128)(2,1)} %bitcast.81, bf16[3,48,8,64]{1,3,2,0:T(8,128)(2,1)} %bitcast.84, bf16[3,48,8,64]{1,3,2,0:T(8,128)(2,1)} %bitcast.80, ...), kind=kOutput, calls=%fused_computation.28 | convolution fusion | flops 32294208 | bytes 2511360 | tf_op jit(solution)/shard_map/bhqk,bkhd->bqhd/dot_general | solution.py:71
  203.7 2.7 multiply_convert_fusion
  207.8 2.2 fusion.10
  211.0 3.3 multiply_reduce_fusion.1
  215.2 218.0 %reduce-scatter.2.cloned.1.call-done = bf16[32,1536]{1,0:T(8,128)(2,1)} async-done(((bf16[1024,1536]{1,0:T(8,128)(2,1)}), bf16[32,1536]{1,0:T(8,128)(2,1)}) %reduce-scatter.2.cloned.1.call-update) | async-done | bytes 98320 | tf_op jit(solution)/shard_map/reduce_scatter | solution.py:175
  433.2 53.1 %all-reduce.7 = f32[32,1536]{1,0:T(8,128)S(1)} all-reduce(bf16[32,1536]{1,0:T(8,128)(2,1)} %reduce-scatter.2.cloned.1.call-done), channel_id=1, replica_groups=mesh['dp'=16,'seq'=32] {'dp'}, use_global_device_ids=true, to_apply=%region_8.9 | all-reduce | flops 49152 | bytes 294912 | tf_op jit(solution)/shard_map/psum | solution.py:186
  (136 shorter events, 29.2 us)
Async XLA Ops:
  7.2 115.9 %copy-start = (bf16[512,1024]{1,0:T(8,128)(2,1)S(1)}, bf16[512,1024]{1,0:T(8,128)(2,1)}, u32[]{:S(2)}) copy-start(bf16[512,1024]{1,0:T(8,128)(2,1)} %param.18) | copy-start | bytes 3145732
  7.2 111.7 %all-gather.2.cloned.1.call-start = ((), (), s32[]{:S(2)}) async-start(), calls=%async_computation.2 | async-start | bytes 3514368 | tf_op jit(solution)/shard_map/all_gather | solution.py:116
  10.8 14.5 %copy-start.33 = (s32[1,1,60]{2,1,0:T(1,128)S(1)}, s32[1,1,60]{2,1,0:T(1,128)}, u32[]{:S(2)}) copy-start(s32[1,1,60]{2,1,0:T(1,128)} %param.14) | copy-start | bytes 724
  10.8 14.8 %copy-start.24 = (bf16[1,144,512]{2,1,0:T(8,128)(2,1)S(1)}, bf16[1,144,512]{2,1,0:T(8,128)(2,1)}, u32[]{:S(2)}) copy-start(bf16[1,144,512]{2,1,0:T(8,128)(2,1)} %param.23) | copy-start | bytes 442372
  10.8 15.8 %copy-start.34 = (s32[1,1,60]{2,1,0:T(1,128)S(1)}, s32[1,1,60]{2,1,0:T(1,128)}, u32[]{:S(2)}) copy-start(s32[1,1,60]{2,1,0:T(1,128)} %param.13) | copy-start | bytes 724
  10.8 112.7 %all-to-all-start = ((bf16[32,32,1536]{2,1,0:T(8,128)(2,1)}), bf16[32,32,1536]{2,1,0:T(8,128)(2,1)}, u32[]{:S(2)}, u32[]{:S(2)}) async-start(bf16[32,32,1536]{2,1,0:T(8,128)(2,1)} %stack.2), calls=%async_computation | async-start | bytes 6291456 | tf_op jit(solution)/shard_map/all_to_all | solution.py:132
  24.0 409.2 %reduce-scatter.2.cloned.1.call-start = ((), (), s32[]{:S(2)}) async-start(), calls=%async_computation.3 | async-start | bytes 3244032 | tf_op jit(solution)/shard_map/reduce_scatter | solution.py:175
  25.7 97.4 %copy-start.22 = (bf16[1,144,1024]{2,1,0:T(8,128)(2,1)S(1)}, bf16[1,144,1024]{2,1,0:T(8,128)(2,1)}, u32[]{:S(2)}) copy-start(bf16[1,144,1024]{2,1,0:T(8,128)(2,1)} %param.12) | copy-start | bytes 884740
  27.6 96.0 %copy-start.25 = (f32[1,1024]{1,0:T(1,128)}, f32[1,1024]{1,0:T(1,128)S(1)}, u32[]{:S(2)}) copy-start(f32[1,1024]{1,0:T(1,128)S(1)} %get-tuple-element.17) | copy-start | bytes 12292
  27.6 96.0 %copy-start.28 = (f32[1,1024]{1,0:T(1,128)}, f32[1,1024]{1,0:T(1,128)S(1)}, u32[]{:S(2)}) copy-start(f32[1,1024]{1,0:T(1,128)S(1)} %get-tuple-element.18) | copy-start | bytes 12292
  123.5 3.2 copy-start.6
  126.8 4.8 collective-permute-start
  129.0 6.8 %collective-permute-start.1 = (bf16[96,1024]{1,0:T(8,128)(2,1)S(1)}, bf16[96,1024]{1,0:T(8,128)(2,1)S(1)}, u32[]{:S(2)}, u32[]{:S(2)}) collective-permute-start(bf16[96,1024]{1,0:T(8,128)(2,1)S(1)} %get-tuple-element.20), channel_id=1, source_target_pairs={{1,0},{2,1},{3,2},{4,3},{5,4},{6,5},{7,6},{8,7},{9,8},{10,9},{11,1... | collective-permute-start | bytes 589832 | tf_op jit(solution)/shard_map/ppermute | solution.py:24
  138.0 3.4 copy-start.9
  138.0 4.3 copy-start.8
  139.3 6.6 %copy-start.18 = (bf16[3,48,1,8,64]{1,4,3,0,2:T(8,128)(2,1)}, bf16[3,48,1,8,64]{1,4,3,0,2:T(8,128)(2,1)S(1)}, u32[]{:S(2)}) copy-start(bf16[3,48,1,8,64]{1,4,3,0,2:T(8,128)(2,1)S(1)} %copy.72) | copy-start | bytes 442372
  144.6 6.7 %copy-start.14 = (bf16[3,48,1,8,64]{1,4,3,0,2:T(8,128)(2,1)}, bf16[3,48,1,8,64]{1,4,3,0,2:T(8,128)(2,1)S(1)}, u32[]{:S(2)}) copy-start(bf16[3,48,1,8,64]{1,4,3,0,2:T(8,128)(2,1)S(1)} %copy.69) | copy-start | bytes 442372
  145.9 3.3 copy-start.20
  149.2 4.1 copy-start.35
  181.8 20.0 %collective-permute-start.2 = (f32[96,1024]{1,0:T(8,128)}, f32[96,1024]{1,0:T(8,128)}, u32[]{:S(2)}, u32[]{:S(2)}) collective-permute-start(f32[96,1024]{1,0:T(8,128)} %slice.152), channel_id=1, source_target_pairs={{1,0},{2,1},{3,2},{4,3},{5,4},{6,5},{7,6},{8,7},{9,8},{10,9},{11,1... | collective-permute-start | bytes 1179656 | tf_op jit(solution)/shard_map/ppermute | solution.py:34
  183.4 7.4 %copy-start.36 = (f32[3,8,48]{2,1,0:T(8,128)S(1)}, f32[3,8,48]{2,1,0:T(8,128)}, u32[]{:S(2)}) copy-start(f32[3,8,48]{2,1,0:T(8,128)} %copy-done.35) | copy-start | bytes 13828
  186.1 15.8 %collective-permute-start.3 = (f32[48,1024]{1,0:T(8,128)}, f32[48,1024]{1,0:T(8,128)}, u32[]{:S(2)}, u32[]{:S(2)}) collective-permute-start(f32[48,1024]{1,0:T(8,128)} %slice.154), channel_id=1, source_target_pairs={{0,1},{1,2},{2,3},{3,4},{4,5},{5,6},{6,7},{7,8},{8,9},{9,10},{10,1... | collective-permute-start | bytes 589832 | tf_op jit(solution)/shard_map/ppermute | solution.py:34
  190.8 10.6 %slice-start = ((f32[6,48,16,64]{3,2,1,0:T(8,128)}), f32[3,48,16,64]{3,2,1,0:T(8,128)S(1)}, s32[]{:S(2)}) async-start(f32[6,48,16,64]{3,2,1,0:T(8,128)} %copy-done.5), calls=%async_computation.4 | async-start | bytes 2359296 | tf_op jit(solution)/shard_map/slice | solution.py:165
  207.8 3.2 copy-start.32
  (22 other events, 35.6 us)
Sparse Core Ops, SparseCore 0:
  11.2 107.7 all-gather.1
  206.7 226.4 reduce-scatter.1
